TPU v7x, 512 devices: a whole 4x4x16 slice. The times are simulated.
512 devices in a mesh: sub: 32 (over z_lo, y, core), cr: 4 (over x), cc: 4 (over z_hi).
Axes of the slice: x: 4, y: 4, z: 16 (z_hi: 4, z_lo: 4; z = z_hi * 4 + z_lo), core: 2. Of those that a mesh axis runs over, the one named last changes fastest.
Arguments:
- stiffness: bfloat16 [128, 1536, 1536], P(('sub', 'cr'), 'cc')
- local_inverse: bfloat16 [128, 1536, 1536], P(('sub', 'cr'), 'cc')
- coarse_basis: bfloat16 [128, 64, 1536], P(('sub', 'cr'), None, 'cc'), may hold values from -0.15625 to 0.15625
- coarse_inverse: bfloat16 [128, 64, 64, 128], P(('sub', 'cr'), None, 'cc')
- loads: float32 [128, 1536, 256], P(('sub', 'cr'), 'cc'), may hold values from -6 to 6
- initial: float32 [128, 1536, 256], P(('sub', 'cr'), 'cc'), may hold values from -6 to 6
- margin_rows: int32 [128, 2, 128], P(('sub', 'cr')), may hold values from 0 to 1535, as said below
- coarse_map: int32 [128], replicated, may hold values from 0 to 127, as said below
Outputs:
- solution: float32 [128, 1536, 256], P(('sub', 'cr'), 'cc')
- residual: float32 [128, 1536, 256], P(('sub', 'cr'), 'cc')
Inputs may be any that keep to these rules, and one draw needn't show every extreme that they name: `margin_rows`: the 256 row numbers of one subdomain are distinct. `coarse_map`: every coarse block number appears once.
All inputs are finite; a program needn't handle non-finite values.
Results may differ from a plain program's by a relative error of at most 0.0095.
Values may be sent and summed in bfloat16 or wider, within the bound.
A program may use at most 64 MiB of HBM per device.

v0:
```python
import jax
import jax.numpy as jnp
from jax import lax
from jax.sharding import PartitionSpec as P

COARSE = 64
ITERS = 2


RELAX = 0.5


def passed_along(block, axis, distance):
    devices = range(lax.axis_size(axis))
    route = [(i - distance, i) for i in devices if i - distance in devices]
    return lax.ppermute(block, axis, route)


def pick_rows(values, indices, offset):
    local_index = indices - offset
    inside = (local_index >= 0) & (local_index < values.shape[0])
    picked = jnp.take(values, jnp.clip(local_index, 0, values.shape[0] - 1), axis=0)
    return jnp.where(inside[:, None], picked, 0.0)


def add_rows(values, indices, offset, addend):
    local_index = indices - offset
    inside = (local_index >= 0) & (local_index < values.shape[0])
    target = jnp.where(inside, local_index, values.shape[0])
    return values.at[target].add(addend, mode="drop")


def neighbour_terms(values, left_index, right_index, offset):
    upward = pick_rows(values, right_index, offset)
    downward = pick_rows(values, left_index, offset)
    from_below = passed_along(upward, ("sub", "cr"), 1)
    from_above = passed_along(downward, ("sub", "cr"), -1)
    return lax.psum((from_below, from_above), "cc")


def assembled(values, terms, left_index, right_index, offset):
    lower_added = add_rows(values, left_index, offset, terms[0])
    return add_rows(lower_added, right_index, offset, terms[1])


def column_fold(matrix, pieces):
    return jnp.dot(matrix, pieces, preferred_element_type=jnp.float32)


def stiffness_apply(stiff_block, rounded):
    return column_fold(stiff_block, lax.all_gather(rounded, "cc", axis=0, tiled=True))


def inverse_apply(inverse_block, rounded):
    return column_fold(inverse_block, lax.all_gather(rounded, "cc", axis=0, tiled=True))


def on_device(
    stiffness, local_inverse, coarse_basis, coarse_inverse, loads, initial, margin_rows, coarse_map
):
    stiff_block = stiffness[0]
    inverse_block = local_inverse[0]
    basis_block = coarse_basis[0]
    load_block = loads[0]
    solution = initial[0]
    own_count = stiff_block.shape[0]
    offset = lax.axis_index("cc") * own_count
    left_index = margin_rows[0, 0]
    right_index = margin_rows[0, 1]
    ordered = jnp.take(coarse_inverse[0], coarse_map, axis=2)
    weights = jnp.transpose(ordered, (0, 2, 1)).reshape(COARSE, -1)

    def residual_of(current):
        product = stiffness_apply(stiff_block, current.astype(jnp.bfloat16))
        difference = load_block - product
        return assembled(
            difference,
            neighbour_terms(difference, left_index, right_index, offset),
            left_index,
            right_index,
            offset,
        )

    for iteration in range(ITERS):
        defect = residual_of(solution)
        rounded = defect.astype(jnp.bfloat16)
        partial_sum = jnp.dot(basis_block, rounded, preferred_element_type=jnp.float32)
        quarter = lax.psum_scatter(partial_sum, "cc", scatter_dimension=0, tiled=True).astype(
            jnp.bfloat16
        )
        partial_value = column_fold(
            weights, lax.all_gather(quarter, ("sub", "cr"), axis=0, tiled=True)
        )
        coarse_value = lax.psum(partial_value, "cc").astype(jnp.bfloat16)
        local_part = inverse_apply(inverse_block, rounded)
        coarse_part = lax.dot_general(
            basis_block, coarse_value, (((0,), (0,)), ((), ())), preferred_element_type=jnp.float32
        )
        combined = local_part + coarse_part
        terms = neighbour_terms(combined, left_index, right_index, offset)
        correction = assembled(combined, terms, left_index, right_index, offset)
        solution = solution + RELAX * correction
    final_residual = residual_of(solution)
    return (solution[None], final_residual[None])


def solution(mesh):
    in_specs = (
        P(("sub", "cr"), "cc", None),
        P(("sub", "cr"), "cc", None),
        P(("sub", "cr"), None, "cc"),
        P(("sub", "cr"), None, "cc", None),
        P(("sub", "cr"), "cc", None),
        P(("sub", "cr"), "cc", None),
        P(("sub", "cr"), None, None),
        P(),
    )
    out_specs = (P(("sub", "cr"), "cc", None), P(("sub", "cr"), "cc", None))
    return jax.shard_map(
        on_device, mesh=mesh, in_specs=in_specs, out_specs=out_specs, check_vma=False
    )
```

profile of v0, /device:TPU:6, one launch (start us, length us, event | category | flops | bytes accessed | tf_op | source)
XLA Modules:
  0.0 1279.9 jit_solution(7120339970187590427)
XLA Ops:
  7.2 0.8 and_bitcast_fusion
  8.1 0.8 compare_and_fusion
  8.8 1.0 bitcast_convert_fusion
  9.9 42.3 %all_gather.21 = bf16[1536,256]{1,0:T(8,128)(2,1)S(1)} all-gather(bf16[384,256]{1,0:T(8,128)(2,1)S(1)} %bitcast_convert_fusion), channel_id=1, replica_groups=mesh['sub'=32,'cr'=4,'cc'=4] {'cc'}, dimensions={0}, use_global_device_ids=true | all-gather | bytes 983040 | tf_op jit(solution)/shard_map/all_gather | solution.py:51
  52.6 0.8 gather_fusion.1
  53.5 1.9 collective-permute-start
  55.4 0.8 gather_fusion.2
  56.3 3.9 collective-permute-start.1
  60.4 3.5 collective-permute-done.1
  64.6 69.8 %all-reduce.19.cloned.1.call-done = (f32[128,256]{1,0:T(8,128)}, f32[128,256]{1,0:T(8,128)}) async-done(((f32[128,256]{1,0:T(8,128)}, f32[128,256]{1,0:T(8,128)}), (f32[128,256]{1,0:T(8,128)}, f32[128,256]{1,0:T(8,128)})) %all-reduce.19.cloned.1.call-update) | async-done | bytes 262160 | tf_op jit(solution)/shard_map/psum | solution.py:38
  134.4 1.8 scatter_fusion
  136.3 1.4 scatter_fusion.1
  137.8 0.8 convolution_bitcast_fusion.3
  138.6 30.4 %reduce-scatter.7.cloned.1.call-done = f32[16,256]{1,0:T(8,128)} async-done(((f32[64,256]{1,0:T(8,128)}), f32[16,256]{1,0:T(8,128)}) %reduce-scatter.7.cloned.1.call-update) | async-done | bytes 16400 | tf_op jit(solution)/shard_map/reduce_scatter | solution.py:88
  169.0 1.3 convert_element_type.29
  172.0 33.6 %all_gather.22 = bf16[1536,256]{1,0:T(8,128)(2,1)} all-gather(bf16[384,256]{1,0:T(8,128)(2,1)S(1)} %convert_element_type.28), channel_id=1, replica_groups=mesh['sub'=32,'cr'=4,'cc'=4] {'cc'}, dimensions={0}, use_global_device_ids=true | all-gather | bytes 983040 | tf_op jit(solution)/shard_map/all_gather | solution.py:55
  205.5 261.7 %all-gather.3.cloned.1.call-done = bf16[2048,256]{1,0:T(8,128)(2,1)} async-done(((bf16[16,256]{1,0:T(8,128)(2,1)}), bf16[2048,256]{1,0:T(8,128)(2,1)}) %all-gather.3.cloned.1.call-update) | async-done | bytes 1048592 | tf_op jit(solution)/shard_map/all_gather | solution.py:92
  467.2 1.5 fusion.22
  468.7 26.1 %psum.86 = bf16[64,256]{1,0:T(8,128)(2,1)S(1)} all-reduce(f32[64,256]{1,0:T(8,128)S(1)} %fusion.22), channel_id=1, replica_groups=mesh['sub'=32,'cr'=4,'cc'=4] {'cc'}, use_global_device_ids=true, to_apply=%region_5.7 | all-reduce | flops 16384 | bytes 98304 | tf_op jit(solution)/shard_map/psum | solution.py:94
  495.0 2.5 fusion.3
  497.5 1.2 copy.44
  498.7 0.8 gather_fusion.4
  499.5 0.8 gather_fusion.3
  500.4 1.9 collective-permute-start.2
  502.4 3.9 collective-permute-start.3
  506.3 1.0 collective-permute-done.2
  507.3 2.6 collective-permute-done.3
  510.6 71.4 %all-reduce.17.cloned.1.call-done = (f32[128,256]{1,0:T(8,128)}, f32[128,256]{1,0:T(8,128)}) async-done(((f32[128,256]{1,0:T(8,128)}, f32[128,256]{1,0:T(8,128)}), (f32[128,256]{1,0:T(8,128)}, f32[128,256]{1,0:T(8,128)})) %all-reduce.17.cloned.1.call-update) | async-done | bytes 262160 | tf_op jit(solution)/shard_map/psum | solution.py:38
  582.0 1.8 scatter_fusion.2
  583.9 1.4 scatter_fusion.3
  585.4 34.0 %all_gather.24 = bf16[1536,256]{1,0:T(8,128)(2,1)S(1)} all-gather(bf16[384,256]{1,0:T(8,128)(2,1)S(1)} %fusion.21), channel_id=1, replica_groups=mesh['sub'=32,'cr'=4,'cc'=4] {'cc'}, dimensions={0}, use_global_device_ids=true | all-gather | bytes 983040 | tf_op jit(solution)/shard_map/all_gather | solution.py:51
  620.6 0.8 gather_fusion.5
  621.6 1.9 collective-permute-start.4
  623.5 3.9 collective-permute-start.5
  627.5 1.0 collective-permute-done.4
  628.5 2.6 collective-permute-done.5
  631.8 70.0 %all-reduce.15.cloned.1.call-done = (f32[128,256]{1,0:T(8,128)}, f32[128,256]{1,0:T(8,128)}) async-done(((f32[128,256]{1,0:T(8,128)}, f32[128,256]{1,0:T(8,128)}), (f32[128,256]{1,0:T(8,128)}, f32[128,256]{1,0:T(8,128)})) %all-reduce.15.cloned.1.call-update) | async-done | bytes 262160 | tf_op jit(solution)/shard_map/psum | solution.py:38
  701.8 1.8 scatter_fusion.4
  703.6 1.4 scatter_fusion.5
  705.1 0.8 convolution_bitcast_fusion.2
  705.9 30.4 %reduce-scatter.9.cloned.1.call-done = f32[16,256]{1,0:T(8,128)} async-done(((f32[64,256]{1,0:T(8,128)}), f32[16,256]{1,0:T(8,128)}) %reduce-scatter.9.cloned.1.call-update) | async-done | bytes 16400 | tf_op jit(solution)/shard_map/reduce_scatter | solution.py:88
  736.3 1.3 convert_element_type.33
  737.7 33.3 %all_gather.25 = bf16[1536,256]{1,0:T(8,128)(2,1)} all-gather(bf16[384,256]{1,0:T(8,128)(2,1)S(1)} %convert_element_type.32), channel_id=1, replica_groups=mesh['sub'=32,'cr'=4,'cc'=4] {'cc'}, dimensions={0}, use_global_device_ids=true | all-gather | bytes 983040 | tf_op jit(solution)/shard_map/all_gather | solution.py:55
  771.1 263.5 %all-gather.5.cloned.1.call-done = bf16[2048,256]{1,0:T(8,128)(2,1)} async-done(((bf16[16,256]{1,0:T(8,128)(2,1)}), bf16[2048,256]{1,0:T(8,128)(2,1)}) %all-gather.5.cloned.1.call-update) | async-done | bytes 1048592 | tf_op jit(solution)/shard_map/all_gather | solution.py:92
  1034.6 1.5 fusion.23
  1036.1 25.0 %psum.91 = bf16[64,256]{1,0:T(8,128)(2,1)S(1)} all-reduce(f32[64,256]{1,0:T(8,128)S(1)} %fusion.23), channel_id=1, replica_groups=mesh['sub'=32,'cr'=4,'cc'=4] {'cc'}, use_global_device_ids=true, to_apply=%region_15.17 | all-reduce | flops 16384 | bytes 98304 | tf_op jit(solution)/shard_map/psum | solution.py:94
  1061.4 2.5 fusion.2
  1063.9 1.2 copy.50
  1066.8 1.9 collective-permute-start.6
  1068.7 3.9 collective-permute-start.7
  1072.7 1.0 collective-permute-done.6
  1073.7 2.7 collective-permute-done.7
  1077.1 71.9 %all-reduce.13.cloned.1.call-done = (f32[128,256]{1,0:T(8,128)}, f32[128,256]{1,0:T(8,128)}) async-done(((f32[128,256]{1,0:T(8,128)}, f32[128,256]{1,0:T(8,128)}), (f32[128,256]{1,0:T(8,128)}, f32[128,256]{1,0:T(8,128)})) %all-reduce.13.cloned.1.call-update) | async-done | bytes 262160 | tf_op jit(solution)/shard_map/psum | solution.py:38
  1148.9 1.8 scatter_fusion.6
  1150.8 1.4 scatter_fusion.7
  1152.3 0.8 fusion.9
  1153.1 33.8 %all_gather.27 = bf16[1536,256]{1,0:T(8,128)(2,1)S(1)} all-gather(bf16[384,256]{1,0:T(8,128)(2,1)S(1)} %get-tuple-element.17), channel_id=1, replica_groups=mesh['sub'=32,'cr'=4,'cc'=4] {'cc'}, dimensions={0}, use_global_device_ids=true | all-gather | bytes 983040 | tf_op jit(solution)/shard_map/all_gather | solution.py:51
  1189.1 1.9 collective-permute-start.8
  1191.1 3.9 collective-permute-start.9
  1195.0 1.0 collective-permute-done.8
  1196.0 2.6 collective-permute-done.9
  1199.2 70.2 %all-reduce.11.cloned.1.call-done = (f32[128,256]{1,0:T(8,128)}, f32[128,256]{1,0:T(8,128)}) async-done(((f32[128,256]{1,0:T(8,128)}, f32[128,256]{1,0:T(8,128)}), (f32[128,256]{1,0:T(8,128)}, f32[128,256]{1,0:T(8,128)})) %all-reduce.11.cloned.1.call-update) | async-done | bytes 262160 | tf_op jit(solution)/shard_map/psum | solution.py:38
  1269.4 1.8 scatter_fusion.8
  1271.2 1.4 scatter_fusion.9
  (107 shorter events, 13.0 us)
Async XLA Ops:
  7.2 45.0 %copy-start = (bf16[1,384,1536]{2,1,0:T(8,128)(2,1)S(1)}, bf16[1,384,1536]{2,1,0:T(8,128)(2,1)}, u32[]{:S(2)}) copy-start(bf16[1,384,1536]{2,1,0:T(8,128)(2,1)} %param.10) | copy-start | bytes 3538948
  7.2 45.0 %copy-start.6 = (f32[1,384,256]{2,1,0:T(8,128)S(1)}, f32[1,384,256]{2,1,0:T(8,128)}, u32[]{:S(2)}) copy-start(f32[1,384,256]{2,1,0:T(8,128)} %param.14) | copy-start | bytes 1179652
  7.2 127.2 %all-reduce.19.cloned.1.call-start = ((), (), s32[]{:S(2)}) async-start(), calls=%async_computation.10 | async-start | bytes 524288 | tf_op jit(solution)/shard_map/psum | solution.py:38
  53.4 11.2 copy-start.26
  53.5 6.9 collective-permute-start
  56.3 7.5 collective-permute-start.1
  60.4 3.5 copy-start.16
  63.8 0.7 copy-start.17
  64.5 104.5 %reduce-scatter.7.cloned.1.call-start = ((), (), s32[]{:S(2)}) async-start(), calls=%async_computation.4 | async-start | bytes 81920 | tf_op jit(solution)/shard_map/reduce_scatter | solution.py:88
  134.4 1.8 copy-start.11
  136.2 1.5 copy-start.9
  136.2 34.2 %copy-start.10 = (bf16[1,64,16,128]{3,2,1,0:T(8,128)(2,1)S(1)}, bf16[1,64,16,128]{3,2,1,0:T(8,128)(2,1)}, u32[]{:S(2)}) copy-start(bf16[1,64,16,128]{3,2,1,0:T(8,128)(2,1)} %param.13) | copy-start | bytes 786436
  137.7 33.3 %copy-start.27 = (s32[128]{0:T(128)S(1)}, s32[128]{0:T(128)}, u32[]{:S(2)}) copy-start(s32[128]{0:T(128)} %param.17) | copy-start | bytes 1540
  138.6 328.6 %all-gather.3.cloned.1.call-start = ((), (), s32[]{:S(2)}) async-start(), calls=%async_computation.2 | async-start | bytes 1056768 | tf_op jit(solution)/shard_map/all_gather | solution.py:92
  170.4 411.6 %all-reduce.17.cloned.1.call-start = ((), (), s32[]{:S(2)}) async-start(), calls=%async_computation.9 | async-start | bytes 524288 | tf_op jit(solution)/shard_map/psum | solution.py:38
  205.5 289.5 %copy-start.2 = (bf16[1,384,1536]{2,1,0:T(8,128)(2,1)S(1)}, bf16[1,384,1536]{2,1,0:T(8,128)(2,1)}, u32[]{:S(2)}) copy-start(bf16[1,384,1536]{2,1,0:T(8,128)(2,1)} %param.11) | copy-start | bytes 3538948
  500.4 6.9 collective-permute-start.2
  502.4 7.5 collective-permute-start.3
  507.3 2.6 copy-start.18
  509.9 0.7 copy-start.22
  510.5 191.2 %all-reduce.15.cloned.1.call-start = ((), (), s32[]{:S(2)}) async-start(), calls=%async_computation.8 | async-start | bytes 524288 | tf_op jit(solution)/shard_map/psum | solution.py:38
  582.0 1.8 copy-start.12
  583.8 1.5 copy-start.4
  585.3 34.0 %copy-start.7 = (f32[1,384,256]{2,1,0:T(8,128)S(1)}, f32[1,384,256]{2,1,0:T(8,128)}, u32[]{:S(2)}) copy-start(f32[1,384,256]{2,1,0:T(8,128)} %param.14) | copy-start | bytes 1179652
  621.6 6.9 collective-permute-start.4
  623.5 7.5 collective-permute-start.5
  628.5 2.6 copy-start.19
  631.0 0.7 copy-start.23
  631.7 104.6 %reduce-scatter.9.cloned.1.call-start = ((), (), s32[]{:S(2)}) async-start(), calls=%async_computation.5 | async-start | bytes 81920 | tf_op jit(solution)/shard_map/reduce_scatter | solution.py:88
  701.8 1.8 copy-start.13
  705.9 328.7 %all-gather.5.cloned.1.call-start = ((), (), s32[]{:S(2)}) async-start(), calls=%async_computation.3 | async-start | bytes 1056768 | tf_op jit(solution)/shard_map/all_gather | solution.py:92
  737.7 411.3 %all-reduce.13.cloned.1.call-start = ((), (), s32[]{:S(2)}) async-start(), calls=%async_computation.7 | async-start | bytes 524288 | tf_op jit(solution)/shard_map/psum | solution.py:38
  771.1 290.3 %copy-start.3 = (bf16[1,384,1536]{2,1,0:T(8,128)(2,1)S(1)}, bf16[1,384,1536]{2,1,0:T(8,128)(2,1)}, u32[]{:S(2)}) copy-start(bf16[1,384,1536]{2,1,0:T(8,128)(2,1)} %param.11) | copy-start | bytes 3538948
  1066.8 6.9 collective-permute-start.6
  1068.7 7.6 collective-permute-start.7
  1073.7 2.7 copy-start.20
  1076.3 0.7 copy-start.24
  1077.0 192.4 %all-reduce.11.cloned.1.call-start = ((), (), s32[]{:S(2)}) async-start(), calls=%async_computation.6 | async-start | bytes 524288 | tf_op jit(solution)/shard_map/psum | solution.py:38
  1148.9 1.8 copy-start.14
  1150.8 1.5 copy-start.5
  1152.3 34.7 %copy-start.8 = (f32[1,384,256]{2,1,0:T(8,128)S(1)}, f32[1,384,256]{2,1,0:T(8,128)}, u32[]{:S(2)}) copy-start(f32[1,384,256]{2,1,0:T(8,128)} %param.14) | copy-start | bytes 1179652
  1189.1 6.9 collective-permute-start.8
  1191.1 7.5 collective-permute-start.9
  1196.0 2.6 copy-start.21
  1198.6 0.6 copy-start.25
  1269.4 1.8 copy-start.15
  1272.7 0.7 copy-start.1
Sparse Core Ops, SparseCore 0:
  64.6 69.7 all-reduce.18
  138.7 30.2 reduce-scatter.6
  171.8 295.3 all-gather.2
  510.7 71.3 all-reduce.16
  631.8 69.8 all-reduce.14
  706.0 30.2 reduce-scatter.8
  739.3 295.2 all-gather.4
  1077.1 71.7 all-reduce.12
  1199.3 69.9 all-reduce.10
where the time goes:
time: 1280 us
  waiting for transfers between devices  957 us (75%)
  blocking collectives  228 us (18%)
  starting transfers between devices  29.6 us (2%)
  other arithmetic  23.7 us (2%)
  local copies, waits for them, and re-layouts  15.2 us (1%)
  between operations  14.5 us (1%)
    all_gather x2, waiting for transfers between devices, on_device(): lax.all_gather(quarter, ('sub', 'cr'), axis=0, tiled=True)  525 us
    psum x5, waiting for transfers between devices, neighbour_terms(): return lax.psum((from_below, from_above), 'cc')  353 us
    all_gather x3, blocking collectives, stiffness_apply(): lax.all_gather(rounded, 'cc', axis=0, tiled=True)  110 us
    all_gather x2, blocking collectives, inverse_apply(): lax.all_gather(rounded, 'cc', axis=0, tiled=True)  66.9 us
    reduce_scatter x2, waiting for transfers between devices, on_device(): lax.psum_scatter(partial_sum, 'cc', scatter_dimension=0, tiled=True)  60.8 us
    psum x2, blocking collectives, on_device(): coarse_value = lax.psum(partial_value, 'cc').astype(jnp.bfloat16)  51.1 us
    ppermute x10, starting transfers between devices, passed_along(): return lax.ppermute(block, axis, route)  29.2 us
  transfers between devices with their start and end apart: 19, of which 19 were waited for; matrix products, arithmetic and copies ran while one was open for 0% of the time, Pallas kernels for 0%

commit v1 on v0

v1 whole, which is shorter than its diff:
```python
import functools

import jax
import jax.numpy as jnp
from jax import lax
from jax.experimental import pallas as pl
from jax.experimental.pallas import tpu as pltpu
from jax.sharding import PartitionSpec as P

COARSE = 64
ITERS = 2
RELAX = 0.5
PARTS = 1
SUB_EXTENTS = (4, 4, 2)
RING = 4
MESH = pl.DeviceIdType.MESH
BF16 = jnp.bfloat16
F32 = jnp.float32


def dot(a, b):
    return jnp.dot(a, b, preferred_element_type=F32)


def dot_nt(a, b):
    return lax.dot_general(a, b, (((1,), (1,)), ((), ())), preferred_element_type=F32)


def kernel(
    extents,
    stiff_hbm,
    inverse_hbm,
    basis_ref,
    weight_ref,
    load_ref,
    init_ref,
    row_ref,
    col_ref,
    sol_ref,
    res_ref,
    k_buf,
    a_buf,
    p_buf,
    pt_buf,
    ap_buf,
    kp_buf,
    bp_buf,
    pb_buf,
    kb_buf,
    bt_buf,
    basis_buf,
    gathered,
    defect,
    update,
    picked,
    coarse_acc,
    margin_out,
    margin_in,
    coarse_all,
    value_out,
    value_own,
    value_in,
    value_all,
    final_out,
    final_in,
    final_sum,
    final_near,
    final_all,
    local_sem,
    send_sem,
    recv_sem,
):
    nz, ny, nc, nx = extents
    own, block = stiff_hbm.shape
    width = load_ref.shape[1] // PARTS
    margin = row_ref.shape[1] // 2
    quarter = COARSE // RING
    piece = margin // RING
    sub = lax.axis_index("sub")
    x = lax.axis_index("cr")
    j = lax.axis_index("cc")
    z = sub // (ny * nc)
    y = lax.rem(sub // nc, ny)
    c = lax.rem(sub, nc)
    domain = sub * nx + x
    domains = nz * ny * nc * nx

    def device(zz, yy, cc, xx, jj):
        return ((zz * ny + yy) * nc + cc, xx, jj)

    def ring(delta):
        return lax.rem(j + delta, RING)

    def ring_device(delta):
        return device(z, y, c, x, ring(delta))

    def domain_device(delta):
        other = lax.rem(domain + delta + domains, domains)
        return (other // nx, lax.rem(other, nx), j)

    axes = {
        "z": (nz, z, lambda v: device(v, y, c, x, j)),
        "y": (ny, y, lambda v: device(z, v, c, x, j)),
        "x": (nx, x, lambda v: device(z, y, c, v, j)),
        "c": (nc, c, lambda v: device(z, y, v, x, j)),
    }

    partners = [ring_device(d) for d in range(1, RING)]
    partners += [domain_device(1), domain_device(-1)]
    for extent, mine, at in axes.values():
        partners += [at(lax.rem(mine + d, extent)) for d in range(1, extent)]

    loads_of_matrices = []
    for jj in range(RING):
        for n, (source, target) in enumerate(((stiff_hbm, k_buf), (inverse_hbm, a_buf))):
            copy = pltpu.make_async_copy(
                source.at[:, pl.ds(jj * own, own)], target.at[jj], local_sem.at[2 * jj + n]
            )
            copy.start()
            loads_of_matrices.append(copy)

    barrier = pltpu.get_barrier_semaphore()
    for partner in partners:
        pl.semaphore_signal(barrier, inc=1, device_id=partner, device_id_type=MESH)
    pl.semaphore_wait(barrier, len(partners))

    slots = [0]
    started = []

    def reserve(count):
        first = slots[0]
        slots[0] += count
        return first

    def remote(source, target, slot, to):
        return pltpu.make_async_remote_copy(
            src_ref=source,
            dst_ref=target,
            send_sem=send_sem.at[slot],
            recv_sem=recv_sem.at[slot],
            device_id=to,
            device_id_type=MESH,
        )

    def send(source, target, slot, to):
        copy = remote(source, target, slot, to)
        copy.start()
        started.append(copy)

    def arrive(landed, slot):
        remote(landed, landed, slot, ring_device(1)).wait_recv()

    class Gather:
        def __init__(self, ref, rows):
            self.ref, self.half, self.slot = ref, rows // 2, reserve(6)

        def at(self, delta, half):
            return self.ref.at[ring(delta), pl.ds(half * self.half, self.half)]

        def start(self):
            right, left, s = ring_device(1), ring_device(3), self.slot
            send(self.at(0, 0), self.at(0, 0), s, right)
            send(self.at(0, 1), self.at(0, 1), s + 1, left)
            send(self.at(0, 1), self.at(0, 1), s + 2, right)
            send(self.at(0, 0), self.at(0, 0), s + 3, left)

        def forward(self):
            s = self.slot
            arrive(self.at(3, 0), s)
            send(self.at(3, 0), self.at(3, 0), s + 4, ring_device(1))
            arrive(self.at(1, 1), s + 1)
            send(self.at(1, 1), self.at(1, 1), s + 5, ring_device(3))

        def near(self):
            arrive(self.at(3, 1), self.slot + 2)
            arrive(self.at(1, 0), self.slot + 3)

        def far(self):
            arrive(self.at(2, 0), self.slot + 4)
            arrive(self.at(2, 1), self.slot + 5)

    def swap(name, ref_at):
        extent, mine, at = axes[name]
        first = reserve(max(extent - 1, 0))
        for d in range(1, extent):
            send(ref_at(mine), ref_at(mine), first + d - 1, at(lax.rem(mine + d, extent)))

        def wait():
            for d in range(1, extent):
                arrive(ref_at(lax.rem(mine + extent - d, extent)), first + d - 1)

        return wait

    def columns(h):
        return slice(h * width, (h + 1) * width)

    def one_hots():
        for jj in range(RING):
            lane = lax.broadcasted_iota(jnp.int32, (2 * margin, own), 1) + jj * own
            p_buf[jj] = jnp.where(col_ref[...] == lane, 1.0, 0.0).astype(BF16)
            row = lax.broadcasted_iota(jnp.int32, (own, 2 * margin), 0) + jj * own
            pt_buf[jj] = jnp.where(row_ref[...] == row, 1.0, 0.0).astype(BF16)

    def margin_columns():
        for source, target in ((k_buf, kp_buf), (a_buf, ap_buf)):
            total = dot(source[0], pt_buf[0])
            for jj in range(1, RING):
                total += dot(source[jj], pt_buf[jj])
            target[...] = total.astype(BF16)

    def own_basis():
        row = lax.broadcasted_iota(jnp.int32, (own, own), 0)
        col = lax.broadcasted_iota(jnp.int32, (own, own), 1)
        identity = jnp.where(row == col, 1.0, 0.0).astype(BF16)
        bt_buf[...] = dot_nt(identity, basis_ref[...]).astype(BF16)

    def basis_rows(jj):
        return basis_buf[jj, pl.ds(pl.multiple_of(j * quarter, quarter), quarter), :]

    def basis_terms():
        total = jnp.zeros((own, COARSE), F32)
        shared = jnp.zeros((2 * margin, COARSE), F32)
        rows = jnp.zeros((quarter, 2 * margin), F32)
        for jj in range(RING):
            total += dot_nt(k_buf[jj], basis_buf[jj])
            shared += dot_nt(p_buf[jj], basis_buf[jj])
            rows += dot(basis_rows(jj), pt_buf[jj])
        high = total.astype(BF16)
        kb_buf[0] = high
        kb_buf[1] = (total - high.astype(F32)).astype(BF16)
        pb_buf[...] = shared.astype(BF16)
        bp_buf[...] = rows.astype(BF16)

    def exchange_margins(step, h, values):
        margin_out[step, h, 0] = values[:margin].astype(BF16)
        margin_out[step, h, 1] = values[margin:].astype(BF16)
        first = reserve(2)
        send(margin_out.at[step, h, 1], margin_in.at[step, h, 0], first, domain_device(1))
        send(margin_out.at[step, h, 0], margin_in.at[step, h, 1], first + 1, domain_device(-1))

        def wait():
            arrive(margin_in.at[step, h, 0], first)
            arrive(margin_in.at[step, h, 1], first + 1)
            below, above = margin_in[step, h, 0], margin_in[step, h, 1]
            return masked(below, above)

        return wait

    def masked(below, above):
        zero = jnp.zeros_like(below)
        below = jnp.where(domain > 0, below, zero)
        above = jnp.where(domain < domains - 1, above, zero)
        return jnp.concatenate([below, above], axis=0)

    def process(h):
        cols = columns(h)
        start_block = gathered.at[0, h]
        gathered[0, h, j] = init_ref[:, cols].astype(BF16)
        gather = Gather(start_block, own)
        gather.start()
        if h == 0:
            for copy in loads_of_matrices:
                copy.wait()
            one_hots()
            margin_columns()
            own_basis()
        yield
        sol_ref[:, cols] = init_ref[:, cols]

        def take_start(delta):
            defect[h] -= dot(k_buf[ring(delta)], gathered[0, h, ring(delta)])

        defect[h] = load_ref[:, cols] - dot(k_buf[j], gathered[0, h, j])
        gather.forward()
        if h == 0:
            basis_gather.append(Gather(basis_buf, COARSE))
            basis_buf[j] = basis_ref[...]
            basis_gather[0].start()
        gather.near()
        take_start(3)
        take_start(1)
        if h == 0:
            basis_gather[0].forward()
        gather.far()
        take_start(2)

        for it in range(ITERS):
            level = 1 + 2 * it
            gathered[level, h, j] = defect[h].astype(BF16)
            gather = Gather(gathered.at[level, h], own)
            gather.start()
            yield
            if it == 0 and h == 0:
                basis_gather[0].near()
                basis_gather[0].far()
                basis_terms()

            def take_defect(delta, first=False, level=level):
                jj = ring(delta)
                part = gathered[level, h, jj]
                terms = (
                    (picked, dot(p_buf[jj], part)),
                    (update, dot(a_buf[jj], part)),
                    (coarse_acc, dot(basis_rows(jj), part)),
                )
                for target, term in terms:
                    if first:
                        target[h] = term
                    else:
                        target[h] += term

            take_defect(0, True)
            gather.forward()
            gather.near()
            take_defect(3)
            take_defect(1)
            gather.far()
            take_defect(2)
            margins = exchange_margins(2 * it, h, picked[h])
            yield
            shared = margins()
            result = coarse_acc[h] + dot(bp_buf[...], shared)
            coarse_all[it, h, c, x, y, z] = result.astype(BF16)
            wait_z = swap("z", lambda v: coarse_all.at[it, h, c, x, y, v])
            update[h] += dot(ap_buf[...], shared)
            level += 1
            gathered[level, h, j] = update[h].astype(BF16)
            gather = Gather(gathered.at[level, h], own)
            gather.start()
            wait_z()
            wait_y = swap("y", lambda v: coarse_all.at[it, h, c, x, v])
            yield

            def take_update(delta, first=False, level=level):
                jj = ring(delta)
                part = gathered[level, h, jj]
                term = dot(p_buf[jj], part)
                if first:
                    picked[h] = term
                else:
                    picked[h] += term
                defect[h] -= RELAX * dot(k_buf[jj], part)

            take_update(0, True)
            wait_y()
            wait_x = swap("x", lambda v: coarse_all.at[it, h, c, v])
            gather.forward()
            wait_x()
            wait_c = swap("c", lambda v: coarse_all.at[it, h, v])
            wait_c()
            everything = coarse_all[it, h].reshape(domains * quarter, width)
            partial = dot(weight_ref[...], everything).reshape(RING, quarter, width)
            value_own[h] = partial
            value_out[it, h] = partial.astype(BF16)
            first = reserve(RING - 1)
            for d in range(1, RING):
                send(
                    value_out.at[it, h, ring(d)],
                    value_in.at[it, h, d - 1],
                    first + d - 1,
                    ring_device(d),
                )
            gather.near()
            take_update(3)
            take_update(1)
            total = value_own[h, j]
            for d in range(1, RING):
                arrive(value_in.at[it, h, d - 1], first + d - 1)
                total += value_in[it, h, d - 1].astype(F32)
            value_all[it, h, j] = total.astype(BF16)
            first = reserve(RING - 1)
            for d in range(1, RING):
                send(
                    value_all.at[it, h, j], value_all.at[it, h, j], first + d - 1, ring_device(d)
                )
            gather.far()
            take_update(2)
            for d in range(1, RING):
                arrive(value_all.at[it, h, ring(RING - d)], first + d - 1)
            value = value_all[it, h].reshape(COARSE, width)
            margins = exchange_margins(2 * it + 1, h, picked[h] + dot(pb_buf[...], value))
            defect[h] -= RELAX * (dot(kb_buf[0], value) + dot(kb_buf[1], value))
            sol_ref[:, cols] += RELAX * (update[h] + dot(bt_buf[...], value))
            yield
            shared = margins()
            defect[h] -= RELAX * dot(kp_buf[...], shared)
            sol_ref[:, cols] += RELAX * dot(pt_buf[j], shared)

        mine = dot(p_buf[j], defect[h].astype(BF16))
        final_out[h, :, 0] = mine[:margin].reshape(RING, piece, width).astype(BF16)
        final_out[h, :, 1] = mine[margin:].reshape(RING, piece, width).astype(BF16)
        first = reserve(RING - 1)
        for d in range(1, RING):
            send(final_out.at[h, ring(d)], final_in.at[h, d - 1], first + d - 1, ring_device(d))
        yield
        total = final_out[h, j].astype(F32)
        for d in range(1, RING):
            arrive(final_in.at[h, d - 1], first + d - 1)
            total += final_in[h, d - 1].astype(F32)
        final_sum[h] = total.astype(BF16)
        first = reserve(2)
        send(final_sum.at[h, 1], final_all.at[h, j, 0], first, domain_device(1))
        send(final_sum.at[h, 0], final_all.at[h, j, 1], first + 1, domain_device(-1))
        yield
        arrive(final_all.at[h, j, 0], first)
        arrive(final_all.at[h, j, 1], first + 1)
        first = reserve(RING - 1)
        for d in range(1, RING):
            send(final_all.at[h, j], final_all.at[h, j], first + d - 1, ring_device(d))
        yield
        for d in range(1, RING):
            arrive(final_all.at[h, ring(RING - d)], first + d - 1)
        shared = masked(
            final_all[h, :, 0].reshape(margin, width), final_all[h, :, 1].reshape(margin, width)
        )
        res_ref[:, cols] = defect[h] + dot(pt_buf[j], shared)

    basis_gather = []
    running = [process(h) for h in range(PARTS)]
    while running:
        for item in list(running):
            try:
                next(item)
            except StopIteration:
                running.remove(item)
    for copy in started:
        copy.wait_send()


def on_device(
    stiffness, local_inverse, coarse_basis, coarse_inverse, loads, initial, margin_rows, coarse_map
):
    nz, ny, nc = SUB_EXTENTS
    nx = lax.axis_size("cr")
    own, block = stiffness.shape[1:]
    rhs = loads.shape[2]
    width = rhs // PARTS
    domains = coarse_map.shape[0]
    quarter = COARSE // RING
    margin = margin_rows.shape[2]
    piece = margin // RING
    order = jnp.transpose(coarse_map.reshape(nz, ny, nc, nx), (2, 3, 1, 0)).reshape(-1)
    ordered = jnp.take(coarse_inverse[0], order, axis=2)
    weights = jnp.transpose(ordered, (0, 2, 1)).reshape(COARSE, -1)
    rows = margin_rows[0].reshape(1, 2 * margin)
    vmem = pl.BlockSpec(memory_space=pltpu.VMEM)
    hbm = pl.BlockSpec(memory_space=pl.ANY)
    slots = 256
    result = pl.pallas_call(
        functools.partial(kernel, (nz, ny, nc, nx)),
        out_shape=(
            jax.ShapeDtypeStruct((own, rhs), F32),
            jax.ShapeDtypeStruct((own, rhs), F32),
        ),
        in_specs=[hbm, hbm] + [vmem] * 6,
        out_specs=(vmem, vmem),
        scratch_shapes=[
            pltpu.VMEM((RING, own, own), BF16),
            pltpu.VMEM((RING, own, own), BF16),
            pltpu.VMEM((RING, 2 * margin, own), BF16),
            pltpu.VMEM((RING, own, 2 * margin), BF16),
            pltpu.VMEM((own, 2 * margin), BF16),
            pltpu.VMEM((own, 2 * margin), BF16),
            pltpu.VMEM((quarter, 2 * margin), BF16),
            pltpu.VMEM((2 * margin, COARSE), BF16),
            pltpu.VMEM((2, own, COARSE), BF16),
            pltpu.VMEM((own, COARSE), BF16),
            pltpu.VMEM((RING, COARSE, own), BF16),
            pltpu.VMEM((1 + 2 * ITERS, PARTS, RING, own, width), BF16),
            pltpu.VMEM((PARTS, own, width), F32),
            pltpu.VMEM((PARTS, own, width), F32),
            pltpu.VMEM((PARTS, 2 * margin, width), F32),
            pltpu.VMEM((PARTS, quarter, width), F32),
            pltpu.VMEM((2 * ITERS, PARTS, 2, margin, width), BF16),
            pltpu.VMEM((2 * ITERS, PARTS, 2, margin, width), BF16),
            pltpu.VMEM((ITERS, PARTS, nc, nx, ny, nz, quarter, width), BF16),
            pltpu.VMEM((ITERS, PARTS, RING, quarter, width), BF16),
            pltpu.VMEM((PARTS, RING, quarter, width), F32),
            pltpu.VMEM((ITERS, PARTS, RING - 1, quarter, width), BF16),
            pltpu.VMEM((ITERS, PARTS, RING, quarter, width), BF16),
            pltpu.VMEM((PARTS, RING, 2, piece, width), BF16),
            pltpu.VMEM((PARTS, RING - 1, 2, piece, width), BF16),
            pltpu.VMEM((PARTS, 2, piece, width), BF16),
            pltpu.VMEM((PARTS, 2, piece, width), BF16),
            pltpu.VMEM((PARTS, RING, 2, piece, width), BF16),
            pltpu.SemaphoreType.DMA((2 * RING,)),
            pltpu.SemaphoreType.DMA((slots,)),
            pltpu.SemaphoreType.DMA((slots,)),
        ],
        compiler_params=pltpu.CompilerParams(
            collective_id=0, has_side_effects=True, vmem_limit_bytes=48 * 1024 * 1024
        ),
    )(
        stiffness[0],
        local_inverse[0],
        coarse_basis[0],
        weights,
        loads[0],
        initial[0],
        rows,
        rows.reshape(2 * margin, 1),
    )
    return (result[0][None], result[1][None])


def solution(mesh):
    in_specs = (
        P(("sub", "cr"), "cc", None),
        P(("sub", "cr"), "cc", None),
        P(("sub", "cr"), None, "cc"),
        P(("sub", "cr"), None, "cc", None),
        P(("sub", "cr"), "cc", None),
        P(("sub", "cr"), "cc", None),
        P(("sub", "cr"), None, None),
        P(),
    )
    out_specs = (P(("sub", "cr"), "cc", None), P(("sub", "cr"), "cc", None))
    return jax.shard_map(
        on_device, mesh=mesh, in_specs=in_specs, out_specs=out_specs, check_vma=False
    )
```

time: 1280 us -> 241 us (0.19)
  the two profiles are of different devices: /device:TPU:6 before, /device:TPU:2 now
where the time goes in v1:
time: 241 us
  Pallas kernels  228 us (95%)
  local copies, waits for them, and re-layouts  9.82 us (4%)
    pallas_call x1, Pallas kernels, on_device(): pl.pallas_call(functools.partial(kernel, (nz, ny, nc, nx)), out_shape=(ja...  228 us

profile of v1, /device:TPU:2, one launch (start us, length us, event | category | flops | bytes accessed | tf_op | source)
XLA Modules:
  0.0 240.8 jit_solution(9952209986555603833)
XLA Ops:
  0.6 0.8 reshape.49
  1.4 0.1 copy.13
  1.5 0.1 reshape.51
  1.7 0.0 copy-start.2
  1.7 0.0 copy-start.3
  1.7 2.3 copy.14
  4.1 0.0 copy-start.5
  4.1 0.0 copy-start
  4.1 0.0 copy-start.1
  4.1 2.7 %gather_fusion = bf16[128,64,16]{1,2,0:T(8,128)(2,1)} fusion(bf16[64,16,128]{0,1,2:T(8,128)(2,1)} %bitcast.26, s32[1024]{0:T(1024)S(1)} %pad_clamp_fusion), kind=kCustom, calls=%fused_computation | custom fusion | bytes 524800 | tf_op jit(solution)/shard_map/jit(_take)/gather | solution.py:443
  6.7 0.1 reshape.50
  6.9 2.0 broadcast_select_fusion
  8.9 1.2 copy.16.weight_ref
  10.1 0.0 copy-done.5
  10.1 0.1 copy.17.col_ref
  10.3 0.0 copy-done.2
  10.3 0.0 copy-done.3
  10.3 0.0 copy-done
  10.3 0.0 copy-done.1
  10.3 0.0 copy-start.4
  10.3 0.8 copy-done.4
  11.1 228.2 %shard_map.95 = (f32[384,256]{1,0:T(8,128)S(1)}, f32[384,256]{1,0:T(8,128)S(1)}) custom-call(bf16[384,1536]{1,0:T(8,128)(2,1)S(1)} %bitcast.16, bf16[384,1536]{1,0:T(8,128)(2,1)S(1)} %bitcast.17, bf16[64,384]{1,0:T(8,128)(2,1)S(1)} %bitcast.22, bf16[64,2048]{1,0:T(8,128)(2,1)S(1)} %copy.16.weight_ref, f32[384,256]{1,0:T(8,128)S(1)} %bitcast.20, ...), custom_call_target="tpu_custom_call" | custom-call | tf_op jit(solution)/shard_map/pallas_call | solution.py:449
  239.3 0.7 copy.20
  240.1 0.7 copy.21
  (3 shorter events, 0.0 us)
Async XLA Ops:
  1.7 8.6 %copy-start.2 = (f32[1,384,256]{2,1,0:T(8,128)S(1)}, f32[1,384,256]{2,1,0:T(8,128)}, u32[]{:S(2)}) copy-start(f32[1,384,256]{2,1,0:T(8,128)} %param.12) | copy-start | bytes 1179652
  1.7 8.6 %copy-start.3 = (f32[1,384,256]{2,1,0:T(8,128)S(1)}, f32[1,384,256]{2,1,0:T(8,128)}, u32[]{:S(2)}) copy-start(f32[1,384,256]{2,1,0:T(8,128)} %param.13) | copy-start | bytes 1179652
  4.1 6.1 %copy-start.5 = (s32[1,2,128]{2,1,0:T(2,128)S(1)}, s32[1,2,128]{2,1,0:T(2,128)}, u32[]{:S(2)}) copy-start(s32[1,2,128]{2,1,0:T(2,128)} %param.14) | copy-start | bytes 3076
  4.1 6.3 %copy-start = (bf16[1,384,1536]{2,1,0:T(8,128)(2,1)S(1)}, bf16[1,384,1536]{2,1,0:T(8,128)(2,1)}, u32[]{:S(2)}) copy-start(bf16[1,384,1536]{2,1,0:T(8,128)(2,1)} %param.8) | copy-start | bytes 3538948
  4.1 6.3 %copy-start.1 = (bf16[1,384,1536]{2,1,0:T(8,128)(2,1)S(1)}, bf16[1,384,1536]{2,1,0:T(8,128)(2,1)}, u32[]{:S(2)}) copy-start(bf16[1,384,1536]{2,1,0:T(8,128)(2,1)} %param.9) | copy-start | bytes 3538948
  10.3 0.8 copy-start.4

commit v2 on v1

--- a/solution.py
+++ b/solution.py
@@ -10,9 +10,19 @@
 COARSE = 64
 ITERS = 2
 RELAX = 0.5
-PARTS = 1
+PARTS = 2
 SUB_EXTENTS = (4, 4, 2)
 RING = 4
+ORDER = (
+    "Ax0", "matrices", "Ax1", "Bx0", "Ax2", "Bx1", "start_basis", "weights", "Ax3", "Ae1",
+    "Bx2", "forward_basis", "Ae2", "Bx3", "Ae3", "end_basis", "Be1", "Ae4", "Au1", "Be2",
+    "Be3", "Au2", "Au3", "Au4", "Au5", "Be4", "Bu1", "Au6", "Au7", "Bu2",
+    "Au8", "Bu3", "Bu4", "Bu5", "Au9", "Bu6", "Bu7", "Bu8", "Ae1", "Bu9",
+    "Ae2", "Ae3", "Be1", "Ae4", "Be2", "Au1", "Be3", "Au2", "Au3", "Be4",
+    "Au4", "Bu1", "Au5", "Au6", "Bu2", "Bu3", "Au7", "Bu4", "Bu5", "Bu6",
+    "Au8", "Bu7", "Bu8", "Au9", "Bu9", "Af1", "Bf1", "Af2", "Bf2", "Af3",
+    "Bf3",
+)
 MESH = pl.DeviceIdType.MESH
 BF16 = jnp.bfloat16
 F32 = jnp.float32
@@ -30,14 +40,19 @@
     extents,
     stiff_hbm,
     inverse_hbm,
-    basis_ref,
-    weight_ref,
+    basis_hbm,
+    coarse_hbm,
+    load_hbm,
+    init_hbm,
+    row_ref,
+    map_ref,
+    sol_ref,
+    res_ref,
     load_ref,
     init_ref,
-    row_ref,
-    col_ref,
-    sol_ref,
-    res_ref,
+    basis_ref,
+    coarse_ref,
+    weight_buf,
     k_buf,
     a_buf,
     p_buf,
@@ -53,14 +68,12 @@
     defect,
     update,
     picked,
-    coarse_acc,
     margin_out,
     margin_in,
     coarse_all,
     value_out,
     value_own,
     value_in,
-    value_all,
     final_out,
     final_in,
     final_sum,
@@ -73,7 +86,7 @@
     nz, ny, nc, nx = extents
     own, block = stiff_hbm.shape
     width = load_ref.shape[1] // PARTS
-    margin = row_ref.shape[1] // 2
+    margin = row_ref.shape[1]
     quarter = COARSE // RING
     piece = margin // RING
     sub = lax.axis_index("sub")
@@ -110,19 +123,23 @@
     for extent, mine, at in axes.values():
         partners += [at(lax.rem(mine + d, extent)) for d in range(1, extent)]
 
-    loads_of_matrices = []
-    for jj in range(RING):
-        for n, (source, target) in enumerate(((stiff_hbm, k_buf), (inverse_hbm, a_buf))):
-            copy = pltpu.make_async_copy(
-                source.at[:, pl.ds(jj * own, own)], target.at[jj], local_sem.at[2 * jj + n]
-            )
-            copy.start()
-            loads_of_matrices.append(copy)
+    copies = []
+
+    def fetch(source, target):
+        copy = pltpu.make_async_copy(source, target, local_sem.at[len(copies)])
+        copy.start()
+        copies.append(copy)
 
     barrier = pltpu.get_barrier_semaphore()
     for partner in partners:
         pl.semaphore_signal(barrier, inc=1, device_id=partner, device_id_type=MESH)
-    pl.semaphore_wait(barrier, len(partners))
+    fetch(init_hbm, init_ref)
+    fetch(load_hbm, load_ref)
+    fetch(basis_hbm, basis_ref)
+    for source, target in ((stiff_hbm, k_buf), (inverse_hbm, a_buf)):
+        for jj in range(RING):
+            fetch(source.at[:, pl.ds(jj * own, own)], target.at[jj])
+    fetch(coarse_hbm, coarse_ref)
 
     slots = [0]
     started = []
@@ -194,12 +211,32 @@
     def columns(h):
         return slice(h * width, (h + 1) * width)
 
+    def equal(a, b):
+        return jnp.where(a == b, 1.0, 0.0).astype(BF16)
+
+    def iota(shape, dim):
+        return lax.broadcasted_iota(jnp.int32, shape, dim)
+
     def one_hots():
+        size = (own, margin)
+        identity = equal(iota((2 * margin,) * 2, 0), iota((2 * margin,) * 2, 1))
         for jj in range(RING):
-            lane = lax.broadcasted_iota(jnp.int32, (2 * margin, own), 1) + jj * own
-            p_buf[jj] = jnp.where(col_ref[...] == lane, 1.0, 0.0).astype(BF16)
-            row = lax.broadcasted_iota(jnp.int32, (own, 2 * margin), 0) + jj * own
-            pt_buf[jj] = jnp.where(row_ref[...] == row, 1.0, 0.0).astype(BF16)
+            row = iota(size, 0) + jj * own
+            pt_buf[jj, :, :margin] = equal(row_ref[0:1, :], row)
+            pt_buf[jj, :, margin:] = equal(row_ref[1:2, :], row)
+            p_buf[jj] = dot_nt(identity, pt_buf[jj]).astype(BF16)
+
+    def order_weights():
+        chunks, rows, lanes = weight_buf.shape
+        select = equal(map_ref[...], iota((domains, domains), 0))
+        ordered = dot(coarse_ref[...].reshape(rows * quarter, domains), select).astype(BF16)
+        for chunk in range(chunks):
+            owner = iota((domains, lanes), 1) // quarter + chunk * (lanes // quarter)
+            wide = dot(ordered, equal(iota((domains, lanes), 0), owner))
+            wide = wide.reshape(rows, quarter, lanes)
+            size = (1, quarter, lanes)
+            keep = iota(size, 1) == lax.rem(iota(size, 2), quarter)
+            weight_buf[chunk] = jnp.sum(jnp.where(keep, wide, 0.0), axis=1).astype(BF16)
 
     def margin_columns():
         for source, target in ((k_buf, kp_buf), (a_buf, ap_buf)):
@@ -209,9 +246,7 @@
             target[...] = total.astype(BF16)
 
     def own_basis():
-        row = lax.broadcasted_iota(jnp.int32, (own, own), 0)
-        col = lax.broadcasted_iota(jnp.int32, (own, own), 1)
-        identity = jnp.where(row == col, 1.0, 0.0).astype(BF16)
+        identity = equal(iota((own, own), 0), iota((own, own), 1))
         bt_buf[...] = dot_nt(identity, basis_ref[...]).astype(BF16)
 
     def basis_rows(jj):
@@ -254,33 +289,22 @@
 
     def process(h):
         cols = columns(h)
-        start_block = gathered.at[0, h]
         gathered[0, h, j] = init_ref[:, cols].astype(BF16)
-        gather = Gather(start_block, own)
+        gather = Gather(gathered.at[0, h], own)
         gather.start()
-        if h == 0:
-            for copy in loads_of_matrices:
-                copy.wait()
-            one_hots()
-            margin_columns()
-            own_basis()
-        yield
         sol_ref[:, cols] = init_ref[:, cols]
+        yield "x0"
 
         def take_start(delta):
             defect[h] -= dot(k_buf[ring(delta)], gathered[0, h, ring(delta)])
 
         defect[h] = load_ref[:, cols] - dot(k_buf[j], gathered[0, h, j])
         gather.forward()
-        if h == 0:
-            basis_gather.append(Gather(basis_buf, COARSE))
-            basis_buf[j] = basis_ref[...]
-            basis_gather[0].start()
+        yield "x1"
         gather.near()
         take_start(3)
         take_start(1)
-        if h == 0:
-            basis_gather[0].forward()
+        yield "x2"
         gather.far()
         take_start(2)
 
@@ -289,20 +313,12 @@
             gathered[level, h, j] = defect[h].astype(BF16)
             gather = Gather(gathered.at[level, h], own)
             gather.start()
-            yield
-            if it == 0 and h == 0:
-                basis_gather[0].near()
-                basis_gather[0].far()
-                basis_terms()
+            yield "x3" if it == 0 else "u9"
 
             def take_defect(delta, first=False, level=level):
                 jj = ring(delta)
                 part = gathered[level, h, jj]
-                terms = (
-                    (picked, dot(p_buf[jj], part)),
-                    (update, dot(a_buf[jj], part)),
-                    (coarse_acc, dot(basis_rows(jj), part)),
-                )
+                terms = ((picked, dot(p_buf[jj], part)), (update, dot(a_buf[jj], part)))
                 for target, term in terms:
                     if first:
                         target[h] = term
@@ -311,25 +327,28 @@
 
             take_defect(0, True)
             gather.forward()
+            yield "e1"
             gather.near()
             take_defect(3)
             take_defect(1)
+            yield "e2"
             gather.far()
             take_defect(2)
             margins = exchange_margins(2 * it, h, picked[h])
-            yield
+            yield "e3"
+            result = dot(basis_rows(0), gathered[level, h, 0])
+            for jj in range(1, RING):
+                result += dot(basis_rows(jj), gathered[level, h, jj])
             shared = margins()
-            result = coarse_acc[h] + dot(bp_buf[...], shared)
-            coarse_all[it, h, c, x, y, z] = result.astype(BF16)
-            wait_z = swap("z", lambda v: coarse_all.at[it, h, c, x, y, v])
+            result += dot(bp_buf[...], shared)
+            coarse_all[it, h, z, y, c, x] = result.astype(BF16)
+            wait = swap("z", lambda v: coarse_all.at[it, h, v, y, c, x])
             update[h] += dot(ap_buf[...], shared)
             level += 1
             gathered[level, h, j] = update[h].astype(BF16)
             gather = Gather(gathered.at[level, h], own)
             gather.start()
-            wait_z()
-            wait_y = swap("y", lambda v: coarse_all.at[it, h, c, x, v])
-            yield
+            yield "e4"
 
             def take_update(delta, first=False, level=level):
                 jj = ring(delta)
@@ -341,47 +360,49 @@
                     picked[h] += term
                 defect[h] -= RELAX * dot(k_buf[jj], part)
 
+            wait()
+            wait = swap("y", lambda v: coarse_all.at[it, h, :, v, c, x])
             take_update(0, True)
-            wait_y()
-            wait_x = swap("x", lambda v: coarse_all.at[it, h, c, v])
+            yield "u1"
+            wait()
+            wait = swap("x", lambda v: coarse_all.at[it, h, :, :, c, v])
+            yield "u2"
             gather.forward()
-            wait_x()
-            wait_c = swap("c", lambda v: coarse_all.at[it, h, v])
-            wait_c()
+            yield "u3"
+            wait()
+            wait = swap("c", lambda v: coarse_all.at[it, h, :, :, v])
+            yield "u4"
+            wait()
             everything = coarse_all[it, h].reshape(domains * quarter, width)
-            partial = dot(weight_ref[...], everything).reshape(RING, quarter, width)
+            chunks, _, lanes = weight_buf.shape
+            partial = dot(weight_buf[0], everything[:lanes])
+            for chunk in range(1, chunks):
+                part = everything[chunk * lanes : (chunk + 1) * lanes]
+                partial += dot(weight_buf[chunk], part)
             value_own[h] = partial
             value_out[it, h] = partial.astype(BF16)
             first = reserve(RING - 1)
-            for d in range(1, RING):
+            for d in (2, 1, 3):
                 send(
-                    value_out.at[it, h, ring(d)],
-                    value_in.at[it, h, d - 1],
-                    first + d - 1,
-                    ring_device(d),
+                    value_out.at[it, h], value_in.at[it, h, d - 1], first + d - 1, ring_device(d)
                 )
+            yield "u5"
             gather.near()
             take_update(3)
             take_update(1)
-            total = value_own[h, j]
+            yield "u6"
+            gather.far()
+            take_update(2)
+            yield "u7"
+            total = value_own[h]
             for d in range(1, RING):
                 arrive(value_in.at[it, h, d - 1], first + d - 1)
                 total += value_in[it, h, d - 1].astype(F32)
-            value_all[it, h, j] = total.astype(BF16)
-            first = reserve(RING - 1)
-            for d in range(1, RING):
-                send(
-                    value_all.at[it, h, j], value_all.at[it, h, j], first + d - 1, ring_device(d)
-                )
-            gather.far()
-            take_update(2)
-            for d in range(1, RING):
-                arrive(value_all.at[it, h, ring(RING - d)], first + d - 1)
-            value = value_all[it, h].reshape(COARSE, width)
+            value = total.astype(BF16)
             margins = exchange_margins(2 * it + 1, h, picked[h] + dot(pb_buf[...], value))
             defect[h] -= RELAX * (dot(kb_buf[0], value) + dot(kb_buf[1], value))
             sol_ref[:, cols] += RELAX * (update[h] + dot(bt_buf[...], value))
-            yield
+            yield "u8"
             shared = margins()
             defect[h] -= RELAX * dot(kp_buf[...], shared)
             sol_ref[:, cols] += RELAX * dot(pt_buf[j], shared)
@@ -390,9 +411,9 @@
         final_out[h, :, 0] = mine[:margin].reshape(RING, piece, width).astype(BF16)
         final_out[h, :, 1] = mine[margin:].reshape(RING, piece, width).astype(BF16)
         first = reserve(RING - 1)
-        for d in range(1, RING):
+        for d in (2, 1, 3):
             send(final_out.at[h, ring(d)], final_in.at[h, d - 1], first + d - 1, ring_device(d))
-        yield
+        yield "u9"
         total = final_out[h, j].astype(F32)
         for d in range(1, RING):
             arrive(final_in.at[h, d - 1], first + d - 1)
@@ -401,28 +422,64 @@
         first = reserve(2)
         send(final_sum.at[h, 1], final_all.at[h, j, 0], first, domain_device(1))
         send(final_sum.at[h, 0], final_all.at[h, j, 1], first + 1, domain_device(-1))
-        yield
+        yield "f1"
         arrive(final_all.at[h, j, 0], first)
         arrive(final_all.at[h, j, 1], first + 1)
         first = reserve(RING - 1)
-        for d in range(1, RING):
+        for d in (2, 1, 3):
             send(final_all.at[h, j], final_all.at[h, j], first + d - 1, ring_device(d))
-        yield
+        yield "f2"
         for d in range(1, RING):
             arrive(final_all.at[h, ring(RING - d)], first + d - 1)
         shared = masked(
             final_all[h, :, 0].reshape(margin, width), final_all[h, :, 1].reshape(margin, width)
         )
         res_ref[:, cols] = defect[h] + dot(pt_buf[j], shared)
-
-    basis_gather = []
-    running = [process(h) for h in range(PARTS)]
-    while running:
-        for item in list(running):
-            try:
-                next(item)
-            except StopIteration:
-                running.remove(item)
+        yield "f3"
+
+    parts = {"A": process(0)}
+    if PARTS > 1:
+        parts["B"] = process(1)
+    basis_gather = Gather(basis_buf, COARSE)
+
+    def fetch_wait(first, last):
+        for copy in copies[first:last]:
+            copy.wait()
+
+    def start_basis():
+        basis_buf[j] = basis_ref[...]
+        basis_gather.start()
+
+    def end_basis():
+        basis_gather.near()
+        basis_gather.far()
+        basis_terms()
+
+    def matrices():
+        fetch_wait(3, 3 + 2 * RING)
+        margin_columns()
+        own_basis()
+
+    def weights():
+        fetch_wait(3 + 2 * RING, 4 + 2 * RING)
+        order_weights()
+
+    extra = {
+        "matrices": matrices,
+        "start_basis": start_basis,
+        "weights": weights,
+        "forward_basis": basis_gather.forward,
+        "end_basis": end_basis,
+    }
+    one_hots()
+    fetch_wait(0, 3)
+    pl.semaphore_wait(barrier, len(partners))
+    for item in ORDER:
+        if item in extra:
+            extra[item]()
+        elif item[0] in parts:
+            if next(parts[item[0]]) != item[1:]:
+                raise ValueError(item)
     for copy in started:
         copy.wait_send()
 
@@ -439,10 +496,7 @@
     quarter = COARSE // RING
     margin = margin_rows.shape[2]
     piece = margin // RING
-    order = jnp.transpose(coarse_map.reshape(nz, ny, nc, nx), (2, 3, 1, 0)).reshape(-1)
-    ordered = jnp.take(coarse_inverse[0], order, axis=2)
-    weights = jnp.transpose(ordered, (0, 2, 1)).reshape(COARSE, -1)
-    rows = margin_rows[0].reshape(1, 2 * margin)
+    lanes = min(256, domains * quarter)
     vmem = pl.BlockSpec(memory_space=pltpu.VMEM)
     hbm = pl.BlockSpec(memory_space=pl.ANY)
     slots = 256
@@ -452,9 +506,14 @@
             jax.ShapeDtypeStruct((own, rhs), F32),
             jax.ShapeDtypeStruct((own, rhs), F32),
         ),
-        in_specs=[hbm, hbm] + [vmem] * 6,
+        in_specs=[hbm] * 6 + [vmem] * 2,
         out_specs=(vmem, vmem),
         scratch_shapes=[
+            pltpu.VMEM((own, rhs), F32),
+            pltpu.VMEM((own, rhs), F32),
+            pltpu.VMEM((COARSE, own), BF16),
+            pltpu.VMEM((COARSE, quarter, domains), BF16),
+            pltpu.VMEM((domains * quarter // lanes, COARSE, lanes), BF16),
             pltpu.VMEM((RING, own, own), BF16),
             pltpu.VMEM((RING, own, own), BF16),
             pltpu.VMEM((RING, 2 * margin, own), BF16),
@@ -470,35 +529,33 @@
             pltpu.VMEM((PARTS, own, width), F32),
             pltpu.VMEM((PARTS, own, width), F32),
             pltpu.VMEM((PARTS, 2 * margin, width), F32),
-            pltpu.VMEM((PARTS, quarter, width), F32),
             pltpu.VMEM((2 * ITERS, PARTS, 2, margin, width), BF16),
             pltpu.VMEM((2 * ITERS, PARTS, 2, margin, width), BF16),
-            pltpu.VMEM((ITERS, PARTS, nc, nx, ny, nz, quarter, width), BF16),
-            pltpu.VMEM((ITERS, PARTS, RING, quarter, width), BF16),
-            pltpu.VMEM((PARTS, RING, quarter, width), F32),
-            pltpu.VMEM((ITERS, PARTS, RING - 1, quarter, width), BF16),
-            pltpu.VMEM((ITERS, PARTS, RING, quarter, width), BF16),
+            pltpu.VMEM((ITERS, PARTS, nz, ny, nc, nx, quarter, width), BF16),
+            pltpu.VMEM((ITERS, PARTS, COARSE, width), BF16),
+            pltpu.VMEM((PARTS, COARSE, width), F32),
+            pltpu.VMEM((ITERS, PARTS, RING - 1, COARSE, width), BF16),
             pltpu.VMEM((PARTS, RING, 2, piece, width), BF16),
             pltpu.VMEM((PARTS, RING - 1, 2, piece, width), BF16),
             pltpu.VMEM((PARTS, 2, piece, width), BF16),
             pltpu.VMEM((PARTS, 2, piece, width), BF16),
             pltpu.VMEM((PARTS, RING, 2, piece, width), BF16),
-            pltpu.SemaphoreType.DMA((2 * RING,)),
+            pltpu.SemaphoreType.DMA((4 + 2 * RING,)),
             pltpu.SemaphoreType.DMA((slots,)),
             pltpu.SemaphoreType.DMA((slots,)),
         ],
         compiler_params=pltpu.CompilerParams(
-            collective_id=0, has_side_effects=True, vmem_limit_bytes=48 * 1024 * 1024
+            collective_id=0, has_side_effects=True, vmem_limit_bytes=60 * 1024 * 1024
         ),
     )(
         stiffness[0],
         local_inverse[0],
         coarse_basis[0],
-        weights,
+        coarse_inverse[0],
         loads[0],
         initial[0],
-        rows,
-        rows.reshape(2 * margin, 1),
+        margin_rows[0],
+        coarse_map.reshape(1, domains),
     )
     return (result[0][None], result[1][None])
 

time: 241 us -> 219 us (0.909)
  Pallas kernels: 228 us -> 214 us
  local copies, waits for them, and re-layouts: 9.82 us -> 3.53 us
    pallas_call x1, Pallas kernels: 228 us -> 214 us  [on_device(): pl.pallas_call(functools.partial(kernel, (nz, ny, nc, nx)), out_shape=(ja...]
    gather x1 -> x0, local copies, waits for them, and re-layouts: 2.67 us -> none  [on_device(): ordered = jnp.take(coarse_inverse[0], order, axis=2)]
where the time goes in v2:
time: 219 us
  Pallas kernels  214 us (98%)
  local copies, waits for them, and re-layouts  3.53 us (2%)
    pallas_call x1, Pallas kernels, on_device(): pl.pallas_call(functools.partial(kernel, (nz, ny, nc, nx)), out_shape=(ja...  214 us

profile of v2, /device:TPU:2, one launch (start us, length us, event | category | flops | bytes accessed | tf_op | source)
XLA Modules:
  0.0 218.5 jit_solution(11263878607546063113)
XLA Ops:
  0.6 214.3 %shard_map.95 = (f32[384,256]{1,0:T(8,128)}, f32[384,256]{1,0:T(8,128)}) custom-call(bf16[384,1536]{1,0:T(8,128)(2,1)} %bitcast.10, bf16[384,1536]{1,0:T(8,128)(2,1)} %bitcast.11, bf16[64,384]{1,0:T(8,128)(2,1)} %bitcast.17, bf16[64,16,128]{2,1,0:T(8,128)(2,1)} %bitcast.16, f32[384,256]{1,0:T(8,128)} %bitcast.14, f32[384,256]{1,0:T(8,128)} %bitcast.15, ...), custom_call_target="tpu_custom_call" | custom-call | tf_op jit(solution)/shard_map/pallas_call | solution.py:503
  215.0 1.8 copy.12
  216.7 1.8 copy.13

commit v3 on v2

--- a/solution.py
+++ b/solution.py
@@ -361,15 +361,20 @@
                 defect[h] -= RELAX * dot(k_buf[jj], part)
 
             wait()
-            wait = swap("y", lambda v: coarse_all.at[it, h, :, v, c, x])
+            low, high = pl.ds(0, nz // 2), pl.ds(nz // 2, nz - nz // 2)
+            wait = swap("y", lambda v: coarse_all.at[it, h, low, v, c, x])
+            other = swap("x", lambda v: coarse_all.at[it, h, high, y, c, v])
             take_update(0, True)
             yield "u1"
             wait()
-            wait = swap("x", lambda v: coarse_all.at[it, h, :, :, c, v])
+            other()
+            wait = swap("x", lambda v: coarse_all.at[it, h, low, :, c, v])
+            other = swap("y", lambda v: coarse_all.at[it, h, high, v, c])
             yield "u2"
             gather.forward()
             yield "u3"
             wait()
+            other()
             wait = swap("c", lambda v: coarse_all.at[it, h, :, :, v])
             yield "u4"
             wait()

time: 219 us -> 218 us (level)
  no operation moved by 1% of the time
where the time goes in v3:
time: 218 us
  Pallas kernels  214 us (98%)
  local copies, waits for them, and re-layouts  3.53 us (2%)
    pallas_call x1, Pallas kernels, on_device(): pl.pallas_call(functools.partial(kernel, (nz, ny, nc, nx)), out_shape=(ja...  214 us

profile of v3, /device:TPU:2, one launch (start us, length us, event | category | flops | bytes accessed | tf_op | source)
XLA Modules:
  0.0 218.0 jit_solution(7190925145233868908)
XLA Ops:
  0.6 213.9 %shard_map.95 = (f32[384,256]{1,0:T(8,128)}, f32[384,256]{1,0:T(8,128)}) custom-call(bf16[384,1536]{1,0:T(8,128)(2,1)} %bitcast.10, bf16[384,1536]{1,0:T(8,128)(2,1)} %bitcast.11, bf16[64,384]{1,0:T(8,128)(2,1)} %bitcast.17, bf16[64,16,128]{2,1,0:T(8,128)(2,1)} %bitcast.16, f32[384,256]{1,0:T(8,128)} %bitcast.14, f32[384,256]{1,0:T(8,128)} %bitcast.15, ...), custom_call_target="tpu_custom_call" | custom-call | tf_op jit(solution)/shard_map/pallas_call | solution.py:508
  214.5 1.8 copy.12
  216.3 1.8 copy.13
